TPU v7x, 1024 devices: a whole 4x8x16 slice. The times are simulated.
1024 devices in a mesh: group: 16 (over z), member: 16 (over y, core), dp: 4 (over x).
Axes of the slice: x: 4, y: 8, z: 16, core: 2. Of those that a mesh axis runs over, the one named last changes fastest.
Arguments:
- out_grad: bfloat16 [24576, 2560], P(('dp', 'group', 'member')), parts along dimension 0, may hold values from -6 to 6
- groups: int32 [24576, 3], P(('dp', 'group', 'member')), parts along dimension 0, may hold values from 0 to 15, all different within a row; in each aligned block of 24 rows (0 to 23, 24 to 47, ...) at most 9 rows name the same one
- picks: int32 [24576, 6], P(('dp', 'group', 'member')), parts along dimension 0, may hold values from 0 to 23, all different within a row
- gates: bfloat16 [24576, 6], P(('dp', 'group', 'member')), parts along dimension 0, may hold values from 0.099609375 to 1
- w_gate: bfloat16 [16, 16, 2560, 384], P('group', 'member'), may hold values from -0.125 to 0.125
- w_up: bfloat16 [16, 16, 2560, 384], P('group', 'member'), may hold values from -0.125 to 0.125
- w_down: bfloat16 [16, 16, 384, 2560], P('group', 'member'), may hold values from -0.21875 to 0.21875
- saved: bfloat16 [16, 16, 1152, 2560], P('group', 'member', 'dp'), parts along dimension 2, may hold values from -6 to 6
Outputs:
- input_grad: bfloat16 [24576, 2560], P(('dp', 'group', 'member')), parts along dimension 0
There are 4 independent parts, one for each index of `dp`. A program takes and returns all parts, laid end to end along the dimension named above; an argument that names none is the same for every part. Nothing has to cross between parts.
Inputs may be any that keep to these rules, and one draw needn't show every extreme that they name: Each row names three different groups; in each aligned block of 24 rows (the rows of one device) no group is named by more than 9 rows, a bound that some block reaches. `picks`: each row names 6 different positions.
All inputs are finite; a program needn't handle non-finite values.
Results may differ from a plain program's by a relative error of at most 0.015.
Values may be sent and summed in bfloat16 or wider, within the bound.
No kernel may reach another device: no remote copies, remote signals or barrier semaphores. Data moves between devices by JAX's collectives and lax.ppermute only.
A program may use at most 32 MiB of HBM per device.

v0:
```python
import jax
import jax.numpy as jnp
from jax import lax
from jax.experimental import pallas as pl
from jax.experimental.pallas import tpu as pltpu
from jax.sharding import PartitionSpec as P

LANES = 128
SUB = 8
WIDE = 16
F32 = jnp.float32
BF16 = jnp.bfloat16


def iota(shape, dim):
    return lax.broadcasted_iota(jnp.int32, shape, dim)


def dot(a, b, left=1, right=0):
    return lax.dot_general(
        a.astype(BF16), b.astype(BF16), (((left,), (right,)), ((), ())), preferred_element_type=F32
    )


def fold(rows):
    return rows.reshape(rows.shape[0], rows.shape[1] // LANES, LANES)


def unfold(rows):
    return rows.reshape(rows.shape[0], rows.shape[1] * LANES)


def pack_group(out_ref, main, ninth, extra):
    count, width = ninth.shape
    half = width // 2
    main = main.reshape(count, SUB, width)
    tiles = half // LANES
    for q in range(tiles):
        low = main[:, :, q * LANES : (q + 1) * LANES]
        high = main[:, :, half + q * LANES : half + (q + 1) * LANES]
        tile = jnp.concatenate([low, high], axis=1)
        out_ref[:, q * WIDE : (q + 1) * WIDE, :] = tile.astype(BF16)
    tail = out_ref.shape[1] - tiles * WIDE
    pad = tail - width // LANES - 1
    block = jnp.concatenate(
        [fold(ninth), extra.reshape(count, 1, LANES), jnp.zeros((count, pad, LANES), F32)], axis=1
    )
    out_ref[:, tiles * WIDE :, :] = block.astype(BF16)


def unpack_group(in_ref, width):
    count = in_ref.shape[0]
    tiles = width // 2 // LANES
    low, high = [], []
    for q in range(tiles):
        tile = in_ref[:, q * WIDE : (q + 1) * WIDE, :].astype(F32)
        low.append(tile[:, :SUB, :].reshape(count * SUB, LANES).astype(BF16))
        high.append(tile[:, SUB:, :].reshape(count * SUB, LANES).astype(BF16))
    main = jnp.concatenate(low + high, axis=1)
    block = in_ref[:, tiles * WIDE :, :].astype(F32)
    ninth = unfold(block[:, : width // LANES, :])
    extra = block[:, width // LANES, :]
    return main, ninth.astype(BF16), extra


def pack_member(out_ref, main, last):
    count = out_ref.shape[0]
    width = main.shape[1]
    tiles = width // LANES
    main = main.astype(BF16).reshape(count, WIDE, width)
    for q in range(tiles):
        out_ref[:, q * WIDE : (q + 1) * WIDE, :] = main[:, :, q * LANES : (q + 1) * LANES]
    room = (out_ref.shape[1] - tiles * WIDE) // 2
    pad = jnp.zeros((count, room - tiles, LANES), F32)
    last = fold(last)
    block = jnp.concatenate([last[:count], pad, last[count:], pad], axis=1)
    out_ref[:, tiles * WIDE :, :] = block.astype(BF16)


def unpack_member(in_ref, width):
    count = in_ref.shape[0]
    tiles = width // LANES
    main = [in_ref[:, q * WIDE : (q + 1) * WIDE, :].reshape(count * WIDE, LANES) for q in range(tiles)]
    main = jnp.concatenate(main, axis=1)
    room = (in_ref.shape[1] - tiles * WIDE) // 2
    block = in_ref[:, tiles * WIDE :, :].astype(F32)
    last = [unfold(block[:, s * room : s * room + tiles, :]) for s in range(2)]
    return main, jnp.concatenate(last, axis=0).astype(BF16)


def columns(rows):
    count = rows.shape[1]
    eye = (iota((count, count), 0) == iota((count, count), 1)).astype(F32)
    return dot(eye, rows.astype(F32), 1, 1)


def place(groups, tok_count, group_count):
    hit = groups[:, 0:1] == iota((tok_count, group_count), 1)
    for k in range(1, 3):
        hit = hit | (groups[:, k : k + 1] == iota((tok_count, group_count), 1))
    hit = hit.astype(F32)
    earlier = (iota((tok_count, tok_count), 1) < iota((tok_count, tok_count), 0)).astype(F32)
    position = jnp.where(hit > 0, dot(earlier, hit), 99.0)
    rows = group_count * SUB
    spread = (iota((rows, group_count), 0) >> 3 == iota((rows, group_count), 1)).astype(F32)
    at = dot(spread, position, 1, 1)
    main = (at == (iota((rows, tok_count), 0) & 7).astype(F32)).astype(F32)
    eye = (iota((group_count, group_count), 0) == iota((group_count, group_count), 1)).astype(F32)
    ninth = (dot(eye, position, 1, 1) == float(SUB)).astype(F32)
    return main, ninth, spread


def send_kernel(
    grad_hbm, groups_hbm, picks_hbm, gates_hbm, out_ref, grad_ref, groups_ref, picks_ref, gates_ref, sems,
    *, group_count,
):
    pairs = (
        (groups_hbm, groups_ref), (picks_hbm, picks_ref), (gates_hbm, gates_ref), (grad_hbm, grad_ref)
    )
    copies = [pltpu.make_async_copy(a, b, sems.at[i]) for i, (a, b) in enumerate(pairs)]
    for copy in copies:
        copy.start()
    for copy in copies[:3]:
        copy.wait()
    tok_count = grad_ref.shape[0]
    groups = columns(groups_ref[...]).astype(jnp.int32)
    picks = columns(picks_ref[...]).astype(jnp.int32)
    gates = columns(gates_ref[...])
    main, ninth, spread = place(groups, tok_count, group_count)
    table = jnp.zeros((tok_count, LANES), F32)
    for k in range(picks.shape[1]):
        pick = picks[:, k : k + 1]
        column = pick >> 3
        group = jnp.where(
            column == 0, groups[:, 0:1], jnp.where(column == 1, groups[:, 1:2], groups[:, 2:3])
        )
        expert = group * SUB + (pick & 7)
        table = table + jnp.where(expert == iota((tok_count, LANES), 1), gates[:, k : k + 1], 0.0)
    rows = group_count * SUB
    lane_of = iota((rows, LANES), 1)
    row_of = iota((rows, LANES), 0)
    same_within = ((iota((LANES, LANES), 0) & 7) == (iota((LANES, LANES), 1) & 7)).astype(F32)
    of_row = jnp.where(row_of >> 3 == lane_of >> 3, dot(main, table), 0.0)
    of_row = jnp.where((row_of & 7) == lane_of >> 3, dot(of_row, same_within), 0.0)
    extra = dot(spread, of_row, 0, 0)
    lane_of = iota((group_count, LANES), 1)
    of_row = jnp.where(iota((group_count, LANES), 0) == lane_of >> 3, dot(ninth, table), 0.0)
    extra = extra + jnp.where(lane_of >> 3 == SUB, dot(of_row, same_within), 0.0)
    copies[3].wait()
    grad = grad_ref[...]
    pack_group(out_ref, dot(main, grad), dot(ninth, grad), extra)


def route_kernel(in_ref, out_ref, main_ref, ninth_ref, *, width, cap):
    count, experts = in_ref.shape[0], SUB
    rows = count * SUB
    main, ninth, extra = unpack_group(in_ref, width)
    spread = (iota((count, rows), 1) >> 3 == iota((count, rows), 0)).astype(F32)
    wide = dot(extra, spread, 0, 0)
    wide = jnp.where(iota((LANES, rows), 0) >> 3 == (iota((LANES, rows), 1) & 7), wide, 0.0)
    pick = ((iota((experts, LANES), 1) & 7) == iota((experts, LANES), 0)).astype(F32)
    gate = dot(pick, wide)
    pick = (iota((experts, LANES), 1) == iota((experts, LANES), 0) + SUB * SUB).astype(F32)
    gate9 = dot(pick, extra, 1, 1)
    on, on9 = (gate > 0).astype(F32), (gate9 > 0).astype(F32)
    mm = (iota((rows, rows), 0) < iota((rows, rows), 1)).astype(F32)
    nm = (iota((count, rows), 0) < iota((count, rows), 1) >> 3).astype(F32)
    mn = (iota((rows, count), 0) >> 3 <= iota((rows, count), 1)).astype(F32)
    nn = (iota((count, count), 0) < iota((count, count), 1)).astype(F32)
    rank = dot(on, mm) + dot(on9, nm)
    rank9 = dot(on, mn) + dot(on9, nn)

    def weights(expert_of, slot_of):
        slots = expert_of.shape[0]
        expand = (expert_of[:, :experts] == iota((slots, experts), 1)).astype(F32)

        def one(rank, gate):
            slot = slot_of[:, : rank.shape[1]].astype(F32)
            value = dot(expand, gate)
            return jnp.where((dot(expand, rank) == slot) & (value > 0), value, 0.0)

        return one(rank, gate), one(rank9, gate9)

    big = iota((experts * WIDE, LANES), 0)
    small = iota((2 * experts, LANES), 0)
    weigh, weigh9 = weights(big >> 4, big & 15)
    last, last9 = weights(small & 7, WIDE + (small >> 3))
    first = dot(weigh, main) + dot(weigh9, ninth)
    second = dot(last, main) + dot(last9, ninth)
    pack_member(out_ref, first, second)
    main_ref[: experts * WIDE, :] = (weigh > 0).astype(F32).astype(BF16)
    main_ref[experts * WIDE :, :] = (last > 0).astype(F32).astype(BF16)
    ninth_ref[: experts * WIDE, :] = (weigh9 > 0).astype(F32).astype(BF16)
    ninth_ref[experts * WIDE :, :] = (last9 > 0).astype(F32).astype(BF16)


def prepare_kernel(flags_ref, *refs, cap):
    saved_hbm, gate_hbm, up_hbm, down_hbm = refs[:4]
    outs, scratch, sems = refs[-16:-11], refs[-11:-1], refs[-1]
    saved_ref, gate_ref, up_ref, down_ref, mine_ref, yours_ref, gate_t, up_t, down_t, _ = scratch

    @pl.when(flags_ref[0] == 1)
    def _():
        pairs = zip((saved_hbm, gate_hbm, up_hbm, down_hbm), (saved_ref, gate_ref, up_ref, down_ref))
        loads = [pltpu.make_async_copy(a, b, sems.at[i]) for i, (a, b) in enumerate(pairs)]
        results = (mine_ref, yours_ref, gate_t, up_t, down_t)
        stores = [
            pltpu.make_async_copy(a, b, sems.at[4 + i]) for i, (a, b) in enumerate(zip(results, outs))
        ]
        for load in loads:
            load.start()
        slots = saved_ref.shape[0]
        half = slots // 2
        experts = half // cap
        core = flags_ref[1]
        row = iota((slots, slots), 0)
        column = jnp.where(row < half, core, 1 - core)
        row = jnp.where(row < half, row, row - half)
        late = row - experts * WIDE
        member = jnp.where(late < 0, row >> 4, late & 7)
        place_in = jnp.where(late < 0, row & 15, WIDE + (late >> 3))
        order = iota((slots, slots), 1) == (2 * member + column) * cap + place_in
        loads[0].wait()
        rows = dot(order.astype(F32), saved_ref[...]).astype(BF16)
        loads[1].wait()
        pre_gate = dot(rows, gate_ref[...])
        loads[2].wait()
        pre_up = dot(rows, up_ref[...])
        gate = 1.0 / (1.0 + jnp.exp(-pre_gate))
        first = pre_up * gate * (1.0 + pre_gate * (1.0 - gate))
        factors = jnp.concatenate([first, pre_gate * gate], axis=1)
        mine_ref[...] = factors[:half]
        yours_ref[...] = factors[half:]
        stores[0].start()
        stores[1].start()
        gate_t[...] = gate_ref[...].T
        stores[2].start()
        up_t[...] = up_ref[...].T
        stores[3].start()
        loads[3].wait()
        down_t[...] = down_ref[...].T
        stores[4].start()
        for store in stores:
            store.wait()


def prepare(flags, inputs, earlier, cap):
    saved, gate, up, down = inputs
    slots, hidden = saved.shape[0], gate.shape[1]
    factor = jax.ShapeDtypeStruct((slots // 2, 2 * hidden), F32)
    outs = [factor, factor] + [
        jax.ShapeDtypeStruct(weight.shape[::-1], BF16) for weight in (gate, up, down)
    ]
    return pl.pallas_call(
        lambda *refs: prepare_kernel(*refs, cap=cap),
        out_shape=[pltpu.HBM(x.shape, x.dtype) for x in outs],
        in_specs=[pl.BlockSpec(memory_space=pltpu.SMEM)] + [HBM] * (4 + len(earlier)),
        out_specs=[HBM] * len(outs),
        scratch_shapes=[pltpu.VMEM(x.shape, x.dtype) for x in (*inputs, *outs)]
        + [pltpu.VMEM((SUB, LANES), F32), pltpu.SemaphoreType.DMA((9,))],
        input_output_aliases={5 + i: i for i in range(len(earlier))},
        cost_estimate=pl.CostEstimate(flops=6 * 10**9, bytes_accessed=20 * 10**6, transcendentals=0),
        compiler_params=pltpu.CompilerParams(vmem_limit_bytes=40 * 1024 * 1024),
    )(flags, *in_hbm(inputs), *in_hbm(earlier))


def expert_kernel(
    in_ref, factor_ref, factor2_ref, down_hbm, down2_hbm, gate_hbm, up_hbm, gate2_hbm, up2_hbm, out_ref,
    down_ref, down2_ref, gate_ref, up_ref, gate2_ref, up2_ref, sems,
):
    width, hidden = down_ref.shape
    sources = (down_hbm, down2_hbm, gate_hbm, up_hbm, gate2_hbm, up2_hbm)
    weights = (down_ref, down2_ref, gate_ref, up_ref, gate2_ref, up2_ref)
    copies = [
        pltpu.make_async_copy(source, weight, sems.at[i])
        for i, (source, weight) in enumerate(zip(sources, weights))
    ]
    for copy in copies:
        copy.start()
    main, last = unpack_member(in_ref, width)
    split = main.shape[0]
    rows = jnp.concatenate([main, last], axis=0)
    sides = []
    for i, factor in enumerate((factor_ref, factor2_ref)):
        copies[i].wait()
        grad = dot(rows, weights[i][...])
        sides.append((grad * factor[:, :hidden]).astype(BF16))
        sides.append((grad * factor[:, hidden:]).astype(BF16))
    for copy in copies[2:]:
        copy.wait()
    parts = dot(sides[0], gate_ref[...])
    for side, weight in zip(sides[1:], (up_ref, gate2_ref, up2_ref)):
        parts = parts + dot(side, weight[...])
    pack_member(out_ref, parts[:split], parts[split:])


def gather_kernel(in_ref, main_ref, ninth_ref, out_ref, *, width):
    main, last = unpack_member(in_ref, width)
    split = main.shape[0]
    total = dot(main_ref[:split, :], main, 0, 0) + dot(main_ref[split:, :], last, 0, 0)
    total9 = dot(ninth_ref[:split, :], main, 0, 0) + dot(ninth_ref[split:, :], last, 0, 0)
    pack_group(out_ref, total, total9, jnp.zeros((out_ref.shape[0], LANES), F32))


def final_kernel(in_ref, groups_ref, out_ref):
    tok_count, width = out_ref.shape
    groups = columns(groups_ref[...]).astype(jnp.int32)
    main, ninth, _ = place(groups, tok_count, in_ref.shape[0])
    rows, rows9, _ = unpack_group(in_ref, width)
    out_ref[...] = (dot(main, rows, 0, 0) + dot(ninth, rows9, 0, 0)).astype(BF16)


HBM = pl.BlockSpec(memory_space=pltpu.HBM)
VMEM = pl.BlockSpec(memory_space=pltpu.VMEM)


def in_hbm(arrays):
    return [pltpu.with_memory_space_constraint(x, pltpu.HBM) for x in arrays]


def call(kernel, outs, *args):
    shapes = [jax.ShapeDtypeStruct(shape, BF16) for shape in outs]
    return pl.pallas_call(
        kernel,
        out_shape=shapes if len(shapes) > 1 else shapes[0],
        compiler_params=pltpu.CompilerParams(vmem_limit_bytes=32 * 1024 * 1024),
    )(*args)


def expert_parts(rows, *weights):
    factors, matrices = weights[:2], in_hbm(weights[2:])
    return pl.pallas_call(
        expert_kernel,
        out_shape=jax.ShapeDtypeStruct(rows.shape, BF16),
        in_specs=[VMEM] * 3 + [HBM] * 6,
        out_specs=VMEM,
        scratch_shapes=[pltpu.VMEM(weight.shape, BF16) for weight in matrices]
        + [pltpu.SemaphoreType.DMA((len(matrices),))],
        compiler_params=pltpu.CompilerParams(vmem_limit_bytes=40 * 1024 * 1024),
    )(rows, *factors, *matrices)


def body(out_grad, groups, picks, gates, w_gate, w_up, w_down, saved):
    group_count = lax.axis_size("group")
    member_count = lax.axis_size("member")
    experts = member_count // 2
    tok_count, width = out_grad.shape
    cap = 12 * tok_count // member_count
    slots = experts * cap
    same_core = [list(range(c, member_count, 2)) for c in range(2)]
    swap = [(i, i ^ 1) for i in range(member_count)]
    core = lax.axis_index("member") % 2
    group_shape = (group_count, width * SUB // LANES + 24, LANES)
    member_shape = (experts, width * WIDE // LANES + 48, LANES)

    def over_group(rows):
        return lax.all_to_all(rows, "group", split_axis=0, concat_axis=0, tiled=True)

    def over_member(rows):
        return lax.all_to_all(
            rows, "member", split_axis=0, concat_axis=0, axis_index_groups=same_core, tiled=True
        )

    def across(rows):
        return lax.ppermute(rows, "member", swap)

    def send(*args):
        return pl.pallas_call(
            lambda *refs: send_kernel(*refs, group_count=group_count),
            out_shape=jax.ShapeDtypeStruct(group_shape, BF16),
            in_specs=[HBM] * len(args),
            out_specs=VMEM,
            scratch_shapes=[pltpu.VMEM(arg.shape, arg.dtype) for arg in args]
            + [pltpu.SemaphoreType.DMA((len(args),))],
            compiler_params=pltpu.CompilerParams(vmem_limit_bytes=32 * 1024 * 1024),
        )(*in_hbm(args))

    w_gate, w_up, w_down, inputs = w_gate[0, 0], w_up[0, 0], w_down[0, 0], saved[0, 0]
    inputs = (inputs, w_gate, w_up, w_down)
    payload = send(out_grad, groups.T, picks.T, gates.T)
    payload, *inputs = lax.optimization_barrier((payload, *inputs))
    earlier = prepare(jnp.stack([core, core]).astype(jnp.int32), inputs, (), cap)
    payload, *earlier = lax.optimization_barrier((payload, *earlier))
    arrived = over_group(payload)
    prepared = prepare(jnp.stack([1 - core, core]).astype(jnp.int32), inputs, tuple(earlier), cap)
    mine, yours, w_gate, w_up, w_down = prepared
    yours, w_down2, w_gate2, w_up2 = [across(x) for x in (yours, w_down, w_gate, w_up)]

    def route(rows):
        kernel = lambda *refs: route_kernel(*refs, width=width, cap=cap)
        return call(
            kernel, [member_shape, (slots, group_count * SUB), (slots, group_count)], rows
        )

    scaled, routing, routing9 = route(arrived)
    weights = (mine, yours, w_down, w_down2, w_gate, w_up, w_gate2, w_up2)
    scaled, *weights = lax.optimization_barrier((scaled,) + weights)
    returned = over_member(expert_parts(over_member(scaled), *weights))
    sums = call(
        lambda *refs: gather_kernel(*refs, width=width),
        [group_shape],
        returned,
        routing,
        routing9,
    )
    return call(final_kernel, [(tok_count, width)], over_group(sums), groups.T)


def solution(mesh):
    token = P(("dp", "group", "member"), None)
    weight = P("group", "member", None, None)
    return jax.shard_map(
        body,
        mesh=mesh,
        in_specs=(token,) * 4 + (weight,) * 3 + (P("group", "member", "dp", None),),
        out_specs=token,
        check_vma=False,
    )
```

profile of v0, /device:TPU:6, one launch (start us, length us, event | category | flops | bytes accessed | tf_op | source)
XLA Modules:
  0.0 172.7 jit_solution(9525409739983768570)
XLA Ops:
  0.0 2.8 %shard_map.82 = bf16[16,184,128]{2,1,0:T(8,128)(2,1)} custom-call(bf16[24,2560]{1,0:T(8,128)(2,1)} %refs_0_.1, s32[3,24]{1,0:T(4,128)} %bitcast.9, s32[6,24]{1,0:T(8,128)} %bitcast.11, bf16[6,24]{1,0:T(8,128)(2,1)} %bitcast.12), custom_call_target="tpu_custom_call" | custom-call | tf_op jit(solution)/shard_map/pallas_call | solution.py:368
  2.8 0.1 pad_add_fusion
  2.9 0.6 shard_map.83
  3.5 18.9 %all-to-all-start = ((bf16[16,184,128]{2,1,0:T(8,128)(2,1)}), bf16[16,184,128]{2,1,0:T(8,128)(2,1)S(1)}, u32[]{:S(2)}, u32[]{:S(2)}) async-start(bf16[16,184,128]{2,1,0:T(8,128)(2,1)} %shard_map.82), calls=%async_computation | async-start | bytes 1507328 | tf_op jit(solution)/shard_map/all_to_all | solution.py:357
  22.4 7.6 %shard_map.85 = (f32[144,768]{1,0:T(8,128)}, f32[144,768]{1,0:T(8,128)}, bf16[384,2560]{1,0:T(8,128)(2,1)}, bf16[384,2560]{1,0:T(8,128)(2,1)}, bf16[2560,384]{1,0:T(8,128)(2,1)}) custom-call(s32[2]{0:T(128)S(1)} %get-tuple-element.72.refs_0_, ...), custom_call_target="tpu_custom_call", output_to_operand_aliasing={{0}: (5, {}), {1}: (6, {}), {2}: (7, {}), {3}: (8, {}), {4}... | custom-call | flops 6000000000 | bytes 20000000 | tf_op jit(solution)/shard_map/pallas_call | solution.py:254
  30.0 0.0 copy-start
  30.0 2.1 %collective-permute-start.1 = (bf16[2560,384]{1,0:T(8,128)(2,1)}, bf16[2560,384]{1,0:T(8,128)(2,1)}, u32[]{:S(2)}, u32[]{:S(2)}) collective-permute-start(bf16[2560,384]{1,0:T(8,128)(2,1)} %get-tuple-element.63.down_hbm), channel_id=1, source_target_pairs={{0,4},{4,0},{8,12},{12,8},{16,20},{20,16},{24,28},{28,24},{32,36},... | collective-permute-start | bytes 5898248 | tf_op jit(solution)/shard_map/ppermute | solution.py:365
  32.1 2.4 %collective-permute-start.2 = (bf16[384,2560]{1,0:T(8,128)(2,1)}, bf16[384,2560]{1,0:T(8,128)(2,1)}, u32[]{:S(2)}, u32[]{:S(2)}) collective-permute-start(bf16[384,2560]{1,0:T(8,128)(2,1)} %get-tuple-element.65.gate_hbm), channel_id=1, source_target_pairs={{0,4},{4,0},{8,12},{12,8},{16,20},{20,16},{24,28},{28,24},{32,36},... | collective-permute-start | bytes 5898248 | tf_op jit(solution)/shard_map/ppermute | solution.py:365
  34.5 1.9 %collective-permute-start.3 = (bf16[384,2560]{1,0:T(8,128)(2,1)}, bf16[384,2560]{1,0:T(8,128)(2,1)}, u32[]{:S(2)}, u32[]{:S(2)}) collective-permute-start(bf16[384,2560]{1,0:T(8,128)(2,1)} %get-tuple-element.66.up_hbm), channel_id=1, source_target_pairs={{0,4},{4,0},{8,12},{12,8},{16,20},{20,16},{24,28},{28,24},{32,36},... | collective-permute-start | bytes 5898248 | tf_op jit(solution)/shard_map/ppermute | solution.py:365
  36.4 2.4 %collective-permute-start = (f32[144,768]{1,0:T(8,128)}, f32[144,768]{1,0:T(8,128)S(1)}, u32[]{:S(2)}, u32[]{:S(2)}) collective-permute-start(f32[144,768]{1,0:T(8,128)} %get-tuple-element.56), channel_id=1, source_target_pairs={{0,4},{4,0},{8,12},{12,8},{16,20},{20,16},{24,28},{28,24},{32,36},... | collective-permute-start | bytes 1327112 | tf_op jit(solution)/shard_map/ppermute | solution.py:365
  38.8 14.3 %all-to-all-done.refs_0_ = bf16[16,184,128]{2,1,0:T(8,128)(2,1)S(1)} async-done(((bf16[16,184,128]{2,1,0:T(8,128)(2,1)}), bf16[16,184,128]{2,1,0:T(8,128)(2,1)S(1)}, u32[]{:S(2)}, u32[]{:S(2)}) %all-to-all-start) | async-done | bytes 753696 | tf_op jit(solution)/shard_map/all_to_all | solution.py:357
  53.1 1.2 shard_map.84
  54.3 0.0 collective-permute-done.factor2_ref
  54.3 0.0 collective-permute-done.1.down2_hbm
  54.3 0.0 collective-permute-done.2.gate2_hbm
  54.3 0.0 collective-permute-done.3.up2_hbm
  54.3 23.6 %all_to_all.20.in_ref = bf16[8,368,128]{2,1,0:T(8,128)(2,1)S(1)} all-to-all(bf16[8,368,128]{2,1,0:T(8,128)(2,1)S(1)} %get-tuple-element.60), channel_id=1, replica_groups={{0,8,16,24,32,40,48,56},{4,12,20,28,36,44,52,60},{1,9,17,25,33,41,49,57..., dimensions={0} | all-to-all | bytes 1507328 | tf_op jit(solution)/shard_map/all_to_all | solution.py:360
  77.9 0.0 copy-done
  77.9 6.2 %shard_map.86 = bf16[8,368,128]{2,1,0:T(8,128)(2,1)S(1)} custom-call(bf16[8,368,128]{2,1,0:T(8,128)(2,1)S(1)} %all_to_all.20.in_ref, f32[144,768]{1,0:T(8,128)S(1)} %copy-done, f32[144,768]{1,0:T(8,128)S(1)} %collective-permute-done.factor2_ref, bf16[2560,384]{1,0:T(8,128)(2,1)} %get-tuple-element.63.down_hbm, ...), custom_call_target="tpu_custom_call" | custom-call | tf_op jit(solution)/shard_map/pallas_call | solution.py:332
  84.1 0.0 copy-start.1
  84.1 20.7 %all_to_all.21.refs_0_ = bf16[8,368,128]{2,1,0:T(8,128)(2,1)S(1)} all-to-all(bf16[8,368,128]{2,1,0:T(8,128)(2,1)S(1)} %shard_map.86), channel_id=1, replica_groups={{0,8,16,24,32,40,48,56},{4,12,20,28,36,44,52,60},{1,9,17,25,33,41,49,57..., dimensions={0} | all-to-all | bytes 1507328 | tf_op jit(solution)/shard_map/all_to_all | solution.py:360
  104.9 0.6 shard_map.87
  105.5 65.8 %all_to_all.22.in_ref = bf16[16,184,128]{2,1,0:T(8,128)(2,1)S(1)} all-to-all(bf16[16,184,128]{2,1,0:T(8,128)(2,1)S(1)} %shard_map.87), channel_id=1, replica_groups=mesh['group'=16,'member'=16,'dp'=4] {'group'}, dimensions={0} | all-to-all | bytes 1507328 | tf_op jit(solution)/shard_map/all_to_all | solution.py:357
  171.3 0.0 copy-done.1
  171.3 1.4 shard_map.88
Async XLA Ops:
  3.5 49.6 %all-to-all-start = ((bf16[16,184,128]{2,1,0:T(8,128)(2,1)}), bf16[16,184,128]{2,1,0:T(8,128)(2,1)S(1)}, u32[]{:S(2)}, u32[]{:S(2)}) async-start(bf16[16,184,128]{2,1,0:T(8,128)(2,1)} %shard_map.82), calls=%async_computation | async-start | bytes 1507328 | tf_op jit(solution)/shard_map/all_to_all | solution.py:357
  30.0 47.9 %copy-start = (f32[144,768]{1,0:T(8,128)S(1)}, f32[144,768]{1,0:T(8,128)}, u32[]{:S(2)}) copy-start(f32[144,768]{1,0:T(8,128)} %get-tuple-element.61.factor_ref) | copy-start | bytes 1327108
  30.0 24.3 %collective-permute-start.1 = (bf16[2560,384]{1,0:T(8,128)(2,1)}, bf16[2560,384]{1,0:T(8,128)(2,1)}, u32[]{:S(2)}, u32[]{:S(2)}) collective-permute-start(bf16[2560,384]{1,0:T(8,128)(2,1)} %get-tuple-element.63.down_hbm), channel_id=1, source_target_pairs={{0,4},{4,0},{8,12},{12,8},{16,20},{20,16},{24,28},{28,24},{32,36},... | collective-permute-start | bytes 5898248 | tf_op jit(solution)/shard_map/ppermute | solution.py:365
  32.1 22.2 %collective-permute-start.2 = (bf16[384,2560]{1,0:T(8,128)(2,1)}, bf16[384,2560]{1,0:T(8,128)(2,1)}, u32[]{:S(2)}, u32[]{:S(2)}) collective-permute-start(bf16[384,2560]{1,0:T(8,128)(2,1)} %get-tuple-element.65.gate_hbm), channel_id=1, source_target_pairs={{0,4},{4,0},{8,12},{12,8},{16,20},{20,16},{24,28},{28,24},{32,36},... | collective-permute-start | bytes 5898248 | tf_op jit(solution)/shard_map/ppermute | solution.py:365
  34.5 19.8 %collective-permute-start.3 = (bf16[384,2560]{1,0:T(8,128)(2,1)}, bf16[384,2560]{1,0:T(8,128)(2,1)}, u32[]{:S(2)}, u32[]{:S(2)}) collective-permute-start(bf16[384,2560]{1,0:T(8,128)(2,1)} %get-tuple-element.66.up_hbm), channel_id=1, source_target_pairs={{0,4},{4,0},{8,12},{12,8},{16,20},{20,16},{24,28},{28,24},{32,36},... | collective-permute-start | bytes 5898248 | tf_op jit(solution)/shard_map/ppermute | solution.py:365
  36.4 17.9 %collective-permute-start = (f32[144,768]{1,0:T(8,128)}, f32[144,768]{1,0:T(8,128)S(1)}, u32[]{:S(2)}, u32[]{:S(2)}) collective-permute-start(f32[144,768]{1,0:T(8,128)} %get-tuple-element.56), channel_id=1, source_target_pairs={{0,4},{4,0},{8,12},{12,8},{16,20},{20,16},{24,28},{28,24},{32,36},... | collective-permute-start | bytes 1327112 | tf_op jit(solution)/shard_map/ppermute | solution.py:365
  84.1 87.2 %copy-start.1 = (s32[24,3]{0,1:T(4,128)S(1)}, s32[24,3]{0,1:T(4,128)}, u32[]{:S(2)}) copy-start(s32[24,3]{0,1:T(4,128)} %param.9) | copy-start | bytes 868
where the time goes:
time: 173 us
  blocking collectives  110 us (64%)
  starting transfers between devices  27.7 us (16%)
  Pallas kernels  20.4 us (12%)
  waiting for transfers between devices  14.3 us (8%)
    all_to_all x1, blocking collectives, over_group(): lax.all_to_all(rows, 'group', split_axis=0, concat_axis=0, tiled=True)  65.8 us
    all_to_all x2, blocking collectives, over_member(): lax.all_to_all(rows, 'member', split_axis=0, concat_axis=0, axis_index_gr...  44.3 us
    all_to_all x1, starting transfers between devices, over_group(): lax.all_to_all(rows, 'group', split_axis=0, concat_axis=0, tiled=True)  18.9 us
    all_to_all x1, waiting for transfers between devices, over_group(): lax.all_to_all(rows, 'group', split_axis=0, concat_axis=0, tiled=True)  14.3 us
    ppermute x4, starting transfers between devices, across(): return lax.ppermute(rows, 'member', swap)  8.79 us
    pallas_call x2, Pallas kernels, prepare(): pl.pallas_call(lambda *refs: prepare_kernel(*refs, cap=cap), out_shape=[p...  8.22 us
    pallas_call x1, Pallas kernels, expert_parts(): pl.pallas_call(expert_kernel, out_shape=jax.ShapeDtypeStruct(rows.shape,...  6.2 us
  transfers between devices with their start and end apart: 5, of which 1 were waited for; matrix products, arithmetic and copies ran while one was open for 0% of the time, Pallas kernels for 5%

commit v1 on v0

--- a/solution.py
+++ b/solution.py
@@ -302,12 +302,17 @@
     pack_group(out_ref, total, total9, jnp.zeros((out_ref.shape[0], LANES), F32))
 
 
-def final_kernel(in_ref, groups_ref, out_ref):
-    tok_count, width = out_ref.shape
+def place_kernel(groups_ref, main_ref, ninth_ref):
     groups = columns(groups_ref[...]).astype(jnp.int32)
-    main, ninth, _ = place(groups, tok_count, in_ref.shape[0])
-    rows, rows9, _ = unpack_group(in_ref, width)
-    out_ref[...] = (dot(main, rows, 0, 0) + dot(ninth, rows9, 0, 0)).astype(BF16)
+    main, ninth, _ = place(groups, main_ref.shape[1], ninth_ref.shape[0])
+    main_ref[...] = main.astype(BF16)
+    ninth_ref[...] = ninth.astype(BF16)
+
+
+def final_kernel(in_ref, main_ref, ninth_ref, out_ref):
+    rows, rows9, _ = unpack_group(in_ref, out_ref.shape[1])
+    total = dot(main_ref[...], rows, 0, 0) + dot(ninth_ref[...], rows9, 0, 0)
+    out_ref[...] = total.astype(BF16)
 
 
 HBM = pl.BlockSpec(memory_space=pltpu.HBM)
@@ -379,10 +384,10 @@
     inputs = (inputs, w_gate, w_up, w_down)
     payload = send(out_grad, groups.T, picks.T, gates.T)
     payload, *inputs = lax.optimization_barrier((payload, *inputs))
-    earlier = prepare(jnp.stack([core, core]).astype(jnp.int32), inputs, (), cap)
+    earlier = prepare(jnp.stack([1 - core, core]).astype(jnp.int32), inputs, (), cap)
     payload, *earlier = lax.optimization_barrier((payload, *earlier))
     arrived = over_group(payload)
-    prepared = prepare(jnp.stack([1 - core, core]).astype(jnp.int32), inputs, tuple(earlier), cap)
+    prepared = prepare(jnp.stack([core, core]).astype(jnp.int32), inputs, tuple(earlier), cap)
     mine, yours, w_gate, w_up, w_down = prepared
     yours, w_down2, w_gate2, w_up2 = [across(x) for x in (yours, w_down, w_gate, w_up)]
 
@@ -403,7 +408,12 @@
         routing,
         routing9,
     )
-    return call(final_kernel, [(tok_count, width)], over_group(sums), groups.T)
+    sums, groups = lax.optimization_barrier((sums, groups.T))
+    back = over_group(sums)
+    placing = call(
+        place_kernel, [(group_count * SUB, tok_count), (group_count, tok_count)], groups
+    )
+    return call(final_kernel, [(tok_count, width)], back, *placing)
 
 
 def solution(mesh):

time: 173 us -> 156 us (0.902)
  blocking collectives: 110 us -> 40.8 us
  waiting for transfers between devices: 14.3 us -> 53.1 us
  starting transfers between devices: 27.7 us -> 40.2 us
    all_to_all x1 -> x0, blocking collectives: 65.8 us -> none  [over_group(): lax.all_to_all(rows, 'group', split_axis=0, concat_axis=0, tiled=True)]
    all_to_all x1 -> x2, waiting for transfers between devices: 14.3 us -> 53.1 us  [over_group(): lax.all_to_all(rows, 'group', split_axis=0, concat_axis=0, tiled=True)]
    all_to_all x1 -> x2, starting transfers between devices: 18.9 us -> 31.4 us  [over_group(): lax.all_to_all(rows, 'group', split_axis=0, concat_axis=0, tiled=True)]
    all_to_all x2, blocking collectives: 44.3 us -> 40.8 us  [over_member(): lax.all_to_all(rows, 'member', split_axis=0, concat_axis=0, axis_index_gr...]
    pallas_call x3 -> x4, Pallas kernels: 3.22 us -> 4.1 us  [call(): pl.pallas_call(kernel, out_shape=shapes if len(shapes) > 1 else shapes[0]...]
  transfers between devices with their start and end apart: 5 -> 6, of which waited for: 1 -> 2; matrix products, arithmetic and copies ran while one was open for 0% -> 0% of each run, Pallas kernels for 5% -> 1%
where the time goes in v1:
time: 156 us
  waiting for transfers between devices  53.1 us (34%)
  blocking collectives  40.8 us (26%)
  starting transfers between devices  40.2 us (26%)
  Pallas kernels  21.3 us (14%)
    all_to_all x2, waiting for transfers between devices, over_group(): lax.all_to_all(rows, 'group', split_axis=0, concat_axis=0, tiled=True)  53.1 us
    all_to_all x2, blocking collectives, over_member(): lax.all_to_all(rows, 'member', split_axis=0, concat_axis=0, axis_index_gr...  40.8 us
    all_to_all x2, starting transfers between devices, over_group(): lax.all_to_all(rows, 'group', split_axis=0, concat_axis=0, tiled=True)  31.4 us
    ppermute x4, starting transfers between devices, across(): return lax.ppermute(rows, 'member', swap)  8.79 us
    pallas_call x2, Pallas kernels, prepare(): pl.pallas_call(lambda *refs: prepare_kernel(*refs, cap=cap), out_shape=[p...  8.2 us
    pallas_call x1, Pallas kernels, expert_parts(): pl.pallas_call(expert_kernel, out_shape=jax.ShapeDtypeStruct(rows.shape,...  6.19 us
    pallas_call x4, Pallas kernels, call(): pl.pallas_call(kernel, out_shape=shapes if len(shapes) > 1 else shapes[0]...  4.1 us
  transfers between devices with their start and end apart: 6, of which 2 were waited for; matrix products, arithmetic and copies ran while one was open for 0% of the time, Pallas kernels for 1%

profile of v1, /device:TPU:6, one launch (start us, length us, event | category | flops | bytes accessed | tf_op | source)
XLA Modules:
  0.0 155.7 jit_solution(850878068386985850)
XLA Ops:
  0.0 2.8 %shard_map.82 = bf16[16,184,128]{2,1,0:T(8,128)(2,1)} custom-call(bf16[24,2560]{1,0:T(8,128)(2,1)} %refs_0_.1, s32[3,24]{1,0:T(4,128)} %bitcast.9, s32[6,24]{1,0:T(8,128)} %bitcast.11, bf16[6,24]{1,0:T(8,128)(2,1)} %bitcast.12), custom_call_target="tpu_custom_call" | custom-call | tf_op jit(solution)/shard_map/pallas_call | solution.py:373
  2.8 0.1 pad_add_fusion
  2.9 7.6 %shard_map.83 = (f32[144,768]{1,0:T(8,128)}, f32[144,768]{1,0:T(8,128)}, bf16[384,2560]{1,0:T(8,128)(2,1)}, bf16[384,2560]{1,0:T(8,128)(2,1)}, bf16[2560,384]{1,0:T(8,128)(2,1)}) custom-call(s32[2]{0:T(128)S(1)} %get-tuple-element.79.refs_0_, bf16[288,2560]{1,0:T(8,128)(2,1)} %bitcast.19, bf16[2560,384]{1,0:T(8,128)(2,1)} %bitcast.13, ...), custom_call_target="tpu_custom_call" | custom-call | flops 6000000000 | bytes 20000000 | tf_op jit(solution)/shard_map/pallas_call | solution.py:254
  10.5 18.9 %all-to-all-start = ((bf16[16,184,128]{2,1,0:T(8,128)(2,1)}), bf16[16,184,128]{2,1,0:T(8,128)(2,1)S(1)}, u32[]{:S(2)}, u32[]{:S(2)}) async-start(bf16[16,184,128]{2,1,0:T(8,128)(2,1)} %shard_map.82), calls=%async_computation | async-start | bytes 1507328 | tf_op jit(solution)/shard_map/all_to_all | solution.py:362
  29.4 0.6 shard_map.85
  30.0 0.0 copy-start
  30.0 2.1 %collective-permute-start.1 = (bf16[2560,384]{1,0:T(8,128)(2,1)}, bf16[2560,384]{1,0:T(8,128)(2,1)}, u32[]{:S(2)}, u32[]{:S(2)}) collective-permute-start(bf16[2560,384]{1,0:T(8,128)(2,1)} %get-tuple-element.67.down_hbm), channel_id=1, source_target_pairs={{0,4},{4,0},{8,12},{12,8},{16,20},{20,16},{24,28},{28,24},{32,36},... | collective-permute-start | bytes 5898248 | tf_op jit(solution)/shard_map/ppermute | solution.py:370
  32.1 2.4 %collective-permute-start.2 = (bf16[384,2560]{1,0:T(8,128)(2,1)}, bf16[384,2560]{1,0:T(8,128)(2,1)}, u32[]{:S(2)}, u32[]{:S(2)}) collective-permute-start(bf16[384,2560]{1,0:T(8,128)(2,1)} %get-tuple-element.69.gate_hbm), channel_id=1, source_target_pairs={{0,4},{4,0},{8,12},{12,8},{16,20},{20,16},{24,28},{28,24},{32,36},... | collective-permute-start | bytes 5898248 | tf_op jit(solution)/shard_map/ppermute | solution.py:370
  34.5 1.9 %collective-permute-start.3 = (bf16[384,2560]{1,0:T(8,128)(2,1)}, bf16[384,2560]{1,0:T(8,128)(2,1)}, u32[]{:S(2)}, u32[]{:S(2)}) collective-permute-start(bf16[384,2560]{1,0:T(8,128)(2,1)} %get-tuple-element.70.up_hbm), channel_id=1, source_target_pairs={{0,4},{4,0},{8,12},{12,8},{16,20},{20,16},{24,28},{28,24},{32,36},... | collective-permute-start | bytes 5898248 | tf_op jit(solution)/shard_map/ppermute | solution.py:370
  36.4 2.4 %collective-permute-start = (f32[144,768]{1,0:T(8,128)}, f32[144,768]{1,0:T(8,128)S(1)}, u32[]{:S(2)}, u32[]{:S(2)}) collective-permute-start(f32[144,768]{1,0:T(8,128)} %get-tuple-element.60), channel_id=1, source_target_pairs={{0,4},{4,0},{8,12},{12,8},{16,20},{20,16},{24,28},{28,24},{32,36},... | collective-permute-start | bytes 1327112 | tf_op jit(solution)/shard_map/ppermute | solution.py:370
  38.8 21.8 %all-to-all-done.refs_0_ = bf16[16,184,128]{2,1,0:T(8,128)(2,1)S(1)} async-done(((bf16[16,184,128]{2,1,0:T(8,128)(2,1)}), bf16[16,184,128]{2,1,0:T(8,128)(2,1)S(1)}, u32[]{:S(2)}, u32[]{:S(2)}) %all-to-all-start) | async-done | bytes 753696 | tf_op jit(solution)/shard_map/all_to_all | solution.py:362
  60.6 1.2 shard_map.84
  61.8 0.0 collective-permute-done.factor2_ref
  61.8 0.0 collective-permute-done.1.down2_hbm
  61.8 0.0 collective-permute-done.2.gate2_hbm
  61.8 0.0 collective-permute-done.3.up2_hbm
  61.8 22.7 %all_to_all.20.in_ref = bf16[8,368,128]{2,1,0:T(8,128)(2,1)S(1)} all-to-all(bf16[8,368,128]{2,1,0:T(8,128)(2,1)S(1)} %get-tuple-element.64), channel_id=1, replica_groups={{0,8,16,24,32,40,48,56},{4,12,20,28,36,44,52,60},{1,9,17,25,33,41,49,57..., dimensions={0} | all-to-all | bytes 1507328 | tf_op jit(solution)/shard_map/all_to_all | solution.py:365
  84.5 0.0 copy-done
  84.5 6.2 %shard_map.86 = bf16[8,368,128]{2,1,0:T(8,128)(2,1)S(1)} custom-call(bf16[8,368,128]{2,1,0:T(8,128)(2,1)S(1)} %all_to_all.20.in_ref, f32[144,768]{1,0:T(8,128)S(1)} %copy-done, f32[144,768]{1,0:T(8,128)S(1)} %collective-permute-done.factor2_ref, bf16[2560,384]{1,0:T(8,128)(2,1)} %get-tuple-element.67.down_hbm, ...), custom_call_target="tpu_custom_call" | custom-call | tf_op jit(solution)/shard_map/pallas_call | solution.py:337
  90.7 0.0 copy-start.1
  90.7 18.2 %all_to_all.21.refs_0_ = bf16[8,368,128]{2,1,0:T(8,128)(2,1)S(1)} all-to-all(bf16[8,368,128]{2,1,0:T(8,128)(2,1)S(1)} %shard_map.86), channel_id=1, replica_groups={{0,8,16,24,32,40,48,56},{4,12,20,28,36,44,52,60},{1,9,17,25,33,41,49,57..., dimensions={0} | all-to-all | bytes 1507328 | tf_op jit(solution)/shard_map/all_to_all | solution.py:365
  108.9 1.5 shard_map.87
  110.4 12.5 %all-to-all-start.3 = ((bf16[16,184,128]{2,1,0:T(8,128)(2,1)}), bf16[16,184,128]{2,1,0:T(8,128)(2,1)S(1)}, u32[]{:S(2)}, u32[]{:S(2)}) async-start(bf16[16,184,128]{2,1,0:T(8,128)(2,1)} %shard_map.87), calls=%async_computation.3 | async-start | bytes 1507328 | tf_op jit(solution)/shard_map/all_to_all | solution.py:362
  122.9 0.0 copy-done.1
  122.9 0.5 shard_map.88
  123.4 31.3 %all-to-all-done.3.in_ref = bf16[16,184,128]{2,1,0:T(8,128)(2,1)S(1)} async-done(((bf16[16,184,128]{2,1,0:T(8,128)(2,1)}), bf16[16,184,128]{2,1,0:T(8,128)(2,1)S(1)}, u32[]{:S(2)}, u32[]{:S(2)}) %all-to-all-start.3) | async-done | bytes 753696 | tf_op jit(solution)/shard_map/all_to_all | solution.py:362
  154.7 1.0 shard_map.89
Async XLA Ops:
  10.5 50.1 %all-to-all-start = ((bf16[16,184,128]{2,1,0:T(8,128)(2,1)}), bf16[16,184,128]{2,1,0:T(8,128)(2,1)S(1)}, u32[]{:S(2)}, u32[]{:S(2)}) async-start(bf16[16,184,128]{2,1,0:T(8,128)(2,1)} %shard_map.82), calls=%async_computation | async-start | bytes 1507328 | tf_op jit(solution)/shard_map/all_to_all | solution.py:362
  30.0 54.5 %copy-start = (f32[144,768]{1,0:T(8,128)S(1)}, f32[144,768]{1,0:T(8,128)}, u32[]{:S(2)}) copy-start(f32[144,768]{1,0:T(8,128)} %get-tuple-element.65.factor_ref) | copy-start | bytes 1327108
  30.0 31.8 %collective-permute-start.1 = (bf16[2560,384]{1,0:T(8,128)(2,1)}, bf16[2560,384]{1,0:T(8,128)(2,1)}, u32[]{:S(2)}, u32[]{:S(2)}) collective-permute-start(bf16[2560,384]{1,0:T(8,128)(2,1)} %get-tuple-element.67.down_hbm), channel_id=1, source_target_pairs={{0,4},{4,0},{8,12},{12,8},{16,20},{20,16},{24,28},{28,24},{32,36},... | collective-permute-start | bytes 5898248 | tf_op jit(solution)/shard_map/ppermute | solution.py:370
  32.1 29.7 %collective-permute-start.2 = (bf16[384,2560]{1,0:T(8,128)(2,1)}, bf16[384,2560]{1,0:T(8,128)(2,1)}, u32[]{:S(2)}, u32[]{:S(2)}) collective-permute-start(bf16[384,2560]{1,0:T(8,128)(2,1)} %get-tuple-element.69.gate_hbm), channel_id=1, source_target_pairs={{0,4},{4,0},{8,12},{12,8},{16,20},{20,16},{24,28},{28,24},{32,36},... | collective-permute-start | bytes 5898248 | tf_op jit(solution)/shard_map/ppermute | solution.py:370
  34.5 27.3 %collective-permute-start.3 = (bf16[384,2560]{1,0:T(8,128)(2,1)}, bf16[384,2560]{1,0:T(8,128)(2,1)}, u32[]{:S(2)}, u32[]{:S(2)}) collective-permute-start(bf16[384,2560]{1,0:T(8,128)(2,1)} %get-tuple-element.70.up_hbm), channel_id=1, source_target_pairs={{0,4},{4,0},{8,12},{12,8},{16,20},{20,16},{24,28},{28,24},{32,36},... | collective-permute-start | bytes 5898248 | tf_op jit(solution)/shard_map/ppermute | solution.py:370
  36.4 25.4 %collective-permute-start = (f32[144,768]{1,0:T(8,128)}, f32[144,768]{1,0:T(8,128)S(1)}, u32[]{:S(2)}, u32[]{:S(2)}) collective-permute-start(f32[144,768]{1,0:T(8,128)} %get-tuple-element.60), channel_id=1, source_target_pairs={{0,4},{4,0},{8,12},{12,8},{16,20},{20,16},{24,28},{28,24},{32,36},... | collective-permute-start | bytes 1327112 | tf_op jit(solution)/shard_map/ppermute | solution.py:370
  90.7 32.2 %copy-start.1 = (s32[24,3]{0,1:T(4,128)S(1)}, s32[24,3]{0,1:T(4,128)}, u32[]{:S(2)}) copy-start(s32[24,3]{0,1:T(4,128)} %param.9) | copy-start | bytes 868
  110.4 44.3 %all-to-all-start.3 = ((bf16[16,184,128]{2,1,0:T(8,128)(2,1)}), bf16[16,184,128]{2,1,0:T(8,128)(2,1)S(1)}, u32[]{:S(2)}, u32[]{:S(2)}) async-start(bf16[16,184,128]{2,1,0:T(8,128)(2,1)} %shard_map.87), calls=%async_computation.3 | async-start | bytes 1507328 | tf_op jit(solution)/shard_map/all_to_all | solution.py:362

commit v2 on v1

--- a/solution.py
+++ b/solution.py
@@ -196,19 +196,22 @@
 
 def prepare_kernel(flags_ref, *refs, cap):
     saved_hbm, gate_hbm, up_hbm, down_hbm = refs[:4]
-    outs, scratch, sems = refs[-16:-11], refs[-11:-1], refs[-1]
-    saved_ref, gate_ref, up_ref, down_ref, mine_ref, yours_ref, gate_t, up_t, down_t, _ = scratch
+    mine_hbm, yours_hbm, gate_t, up_t, down_t = refs[-12:-7]
+    saved_ref, tall_ref, wide_ref, mine_ref, yours_ref, factor_sems, sems = refs[-7:]
 
     @pl.when(flags_ref[0] == 1)
     def _():
-        pairs = zip((saved_hbm, gate_hbm, up_hbm, down_hbm), (saved_ref, gate_ref, up_ref, down_ref))
-        loads = [pltpu.make_async_copy(a, b, sems.at[i]) for i, (a, b) in enumerate(pairs)]
-        results = (mine_ref, yours_ref, gate_t, up_t, down_t)
-        stores = [
-            pltpu.make_async_copy(a, b, sems.at[4 + i]) for i, (a, b) in enumerate(zip(results, outs))
-        ]
-        for load in loads:
-            load.start()
+        def load(source, target):
+            return pltpu.make_async_copy(source, target, sems.at[0])
+
+        def store(source, target):
+            return pltpu.make_async_copy(source, target, sems.at[1])
+
+        first_load = pltpu.make_async_copy(saved_hbm, saved_ref, factor_sems.at[0])
+        first_load.start()
+        gate_load, up_load = load(gate_hbm, tall_ref), load(up_hbm, tall_ref)
+        down_load = load(down_hbm, wide_ref)
+        gate_load.start()
         slots = saved_ref.shape[0]
         half = slots // 2
         experts = half // cap
@@ -220,28 +223,40 @@
         member = jnp.where(late < 0, row >> 4, late & 7)
         place_in = jnp.where(late < 0, row & 15, WIDE + (late >> 3))
         order = iota((slots, slots), 1) == (2 * member + column) * cap + place_in
-        loads[0].wait()
+        first_load.wait()
         rows = dot(order.astype(F32), saved_ref[...]).astype(BF16)
-        loads[1].wait()
-        pre_gate = dot(rows, gate_ref[...])
-        loads[2].wait()
-        pre_up = dot(rows, up_ref[...])
+        gate_load.wait()
+        pre_gate = dot(rows, tall_ref[...])
+        wide_ref[...] = tall_ref[...].T
+        gate_store = store(wide_ref, gate_t)
+        gate_store.start()
+        up_load.start()
+        up_load.wait()
+        pre_up = dot(rows, tall_ref[...])
         gate = 1.0 / (1.0 + jnp.exp(-pre_gate))
         first = pre_up * gate * (1.0 + pre_gate * (1.0 - gate))
         factors = jnp.concatenate([first, pre_gate * gate], axis=1)
         mine_ref[...] = factors[:half]
         yours_ref[...] = factors[half:]
-        stores[0].start()
-        stores[1].start()
-        gate_t[...] = gate_ref[...].T
-        stores[2].start()
-        up_t[...] = up_ref[...].T
-        stores[3].start()
-        loads[3].wait()
-        down_t[...] = down_ref[...].T
-        stores[4].start()
-        for store in stores:
-            store.wait()
+        stores = [
+            pltpu.make_async_copy(mine_ref, mine_hbm, factor_sems.at[1]),
+            pltpu.make_async_copy(yours_ref, yours_hbm, factor_sems.at[2]),
+        ]
+        for one in stores:
+            one.start()
+        gate_store.wait()
+        wide_ref[...] = tall_ref[...].T
+        up_store = store(wide_ref, up_t)
+        up_store.start()
+        up_store.wait()
+        down_load.start()
+        down_load.wait()
+        tall_ref[...] = wide_ref[...].T
+        down_store = store(tall_ref, down_t)
+        down_store.start()
+        down_store.wait()
+        for one in stores:
+            one.wait()
 
 
 def prepare(flags, inputs, earlier, cap):
@@ -256,8 +271,8 @@
         out_shape=[pltpu.HBM(x.shape, x.dtype) for x in outs],
         in_specs=[pl.BlockSpec(memory_space=pltpu.SMEM)] + [HBM] * (4 + len(earlier)),
         out_specs=[HBM] * len(outs),
-        scratch_shapes=[pltpu.VMEM(x.shape, x.dtype) for x in (*inputs, *outs)]
-        + [pltpu.VMEM((SUB, LANES), F32), pltpu.SemaphoreType.DMA((9,))],
+        scratch_shapes=[pltpu.VMEM(x.shape, x.dtype) for x in (saved, gate, down, factor, factor)]
+        + [pltpu.SemaphoreType.DMA((3,)), pltpu.SemaphoreType.DMA((2,))],
         input_output_aliases={5 + i: i for i in range(len(earlier))},
         cost_estimate=pl.CostEstimate(flops=6 * 10**9, bytes_accessed=20 * 10**6, transcendentals=0),
         compiler_params=pltpu.CompilerParams(vmem_limit_bytes=40 * 1024 * 1024),
@@ -286,10 +301,10 @@
         grad = dot(rows, weights[i][...])
         sides.append((grad * factor[:, :hidden]).astype(BF16))
         sides.append((grad * factor[:, hidden:]).astype(BF16))
-    for copy in copies[2:]:
+    copies[2].wait()
+    parts = dot(sides[0], gate_ref[...])
+    for side, weight, copy in zip(sides[1:], (up_ref, gate2_ref, up2_ref), copies[3:]):
         copy.wait()
-    parts = dot(sides[0], gate_ref[...])
-    for side, weight in zip(sides[1:], (up_ref, gate2_ref, up2_ref)):
         parts = parts + dot(side, weight[...])
     pack_member(out_ref, parts[:split], parts[split:])
 

time: 156 us -> 146 us (0.936)
  waiting for transfers between devices: 53.1 us -> 44.4 us
  starting transfers between devices: 40.2 us -> 33.5 us
  Pallas kernels: 21.3 us -> 25 us
  blocking collectives: 40.8 us -> 42.4 us
    all_to_all x2, waiting for transfers between devices: 53.1 us -> 44.3 us  [over_group(): lax.all_to_all(rows, 'group', split_axis=0, concat_axis=0, tiled=True)]
    all_to_all x2, starting transfers between devices: 31.4 us -> 24.7 us  [over_group(): lax.all_to_all(rows, 'group', split_axis=0, concat_axis=0, tiled=True)]
    pallas_call x2, Pallas kernels: 8.2 us -> 12.8 us  [prepare(): pl.pallas_call(lambda *refs: prepare_kernel(*refs, cap=cap), out_shape=[p...]
    all_to_all x2, blocking collectives: 40.8 us -> 42.4 us  [over_member(): lax.all_to_all(rows, 'member', split_axis=0, concat_axis=0, axis_index_gr...]
  transfers between devices with their start and end apart: 6 -> 6, of which waited for: 2 -> 2; matrix products, arithmetic and copies ran while one was open for 0% -> 0% of each run, Pallas kernels for 1% -> 2%
where the time goes in v2:
time: 146 us
  waiting for transfers between devices  44.4 us (30%)
  blocking collectives  42.4 us (29%)
  starting transfers between devices  33.5 us (23%)
  Pallas kernels  25 us (17%)
    all_to_all x2, waiting for transfers between devices, over_group(): lax.all_to_all(rows, 'group', split_axis=0, concat_axis=0, tiled=True)  44.3 us
    all_to_all x2, blocking collectives, over_member(): lax.all_to_all(rows, 'member', split_axis=0, concat_axis=0, axis_index_gr...  42.4 us
    all_to_all x2, starting transfers between devices, over_group(): lax.all_to_all(rows, 'group', split_axis=0, concat_axis=0, tiled=True)  24.7 us
    pallas_call x2, Pallas kernels, prepare(): pl.pallas_call(lambda *refs: prepare_kernel(*refs, cap=cap), out_shape=[p...  12.8 us
    ppermute x4, starting transfers between devices, across(): return lax.ppermute(rows, 'member', swap)  8.79 us
    pallas_call x1, Pallas kernels, expert_parts(): pl.pallas_call(expert_kernel, out_shape=jax.ShapeDtypeStruct(rows.shape,...  5.28 us
    pallas_call x4, Pallas kernels, call(): pl.pallas_call(kernel, out_shape=shapes if len(shapes) > 1 else shapes[0]...  4.11 us
  transfers between devices with their start and end apart: 6, of which 2 were waited for; matrix products, arithmetic and copies ran while one was open for 0% of the time, Pallas kernels for 2%

profile of v2, /device:TPU:6, one launch (start us, length us, event | category | flops | bytes accessed | tf_op | source)
XLA Modules:
  0.0 145.5 jit_solution(4123617056641189593)
XLA Ops:
  0.0 2.8 %shard_map.82 = bf16[16,184,128]{2,1,0:T(8,128)(2,1)} custom-call(bf16[24,2560]{1,0:T(8,128)(2,1)} %refs_0_.1, s32[3,24]{1,0:T(4,128)} %bitcast.9, s32[6,24]{1,0:T(8,128)} %bitcast.11, bf16[6,24]{1,0:T(8,128)(2,1)} %bitcast.12), custom_call_target="tpu_custom_call" | custom-call | tf_op jit(solution)/shard_map/pallas_call | solution.py:388
  2.8 0.1 pad_add_fusion
  2.9 12.2 %shard_map.83 = (f32[144,768]{1,0:T(8,128)}, f32[144,768]{1,0:T(8,128)}, bf16[384,2560]{1,0:T(8,128)(2,1)}, bf16[384,2560]{1,0:T(8,128)(2,1)}, bf16[2560,384]{1,0:T(8,128)(2,1)}) custom-call(s32[2]{0:T(128)S(1)} %get-tuple-element.79.refs_0_, bf16[288,2560]{1,0:T(8,128)(2,1)} %bitcast.19, bf16[2560,384]{1,0:T(8,128)(2,1)} %bitcast.13, ...), custom_call_target="tpu_custom_call" | custom-call | flops 6000000000 | bytes 20000000 | tf_op jit(solution)/shard_map/pallas_call | solution.py:269
  15.1 18.9 %all-to-all-start = ((bf16[16,184,128]{2,1,0:T(8,128)(2,1)}), bf16[16,184,128]{2,1,0:T(8,128)(2,1)S(1)}, u32[]{:S(2)}, u32[]{:S(2)}) async-start(bf16[16,184,128]{2,1,0:T(8,128)(2,1)} %shard_map.82), calls=%async_computation | async-start | bytes 1507328 | tf_op jit(solution)/shard_map/all_to_all | solution.py:377
  34.0 0.6 shard_map.85
  34.6 0.0 copy-start
  34.6 2.1 %collective-permute-start.1 = (bf16[2560,384]{1,0:T(8,128)(2,1)}, bf16[2560,384]{1,0:T(8,128)(2,1)}, u32[]{:S(2)}, u32[]{:S(2)}) collective-permute-start(bf16[2560,384]{1,0:T(8,128)(2,1)} %get-tuple-element.67.down_hbm), channel_id=1, source_target_pairs={{0,4},{4,0},{8,12},{12,8},{16,20},{20,16},{24,28},{28,24},{32,36},... | collective-permute-start | bytes 5898248 | tf_op jit(solution)/shard_map/ppermute | solution.py:385
  36.7 2.4 %collective-permute-start.2 = (bf16[384,2560]{1,0:T(8,128)(2,1)}, bf16[384,2560]{1,0:T(8,128)(2,1)}, u32[]{:S(2)}, u32[]{:S(2)}) collective-permute-start(bf16[384,2560]{1,0:T(8,128)(2,1)} %get-tuple-element.69.gate_hbm), channel_id=1, source_target_pairs={{0,4},{4,0},{8,12},{12,8},{16,20},{20,16},{24,28},{28,24},{32,36},... | collective-permute-start | bytes 5898248 | tf_op jit(solution)/shard_map/ppermute | solution.py:385
  39.1 1.9 %collective-permute-start.3 = (bf16[384,2560]{1,0:T(8,128)(2,1)}, bf16[384,2560]{1,0:T(8,128)(2,1)}, u32[]{:S(2)}, u32[]{:S(2)}) collective-permute-start(bf16[384,2560]{1,0:T(8,128)(2,1)} %get-tuple-element.70.up_hbm), channel_id=1, source_target_pairs={{0,4},{4,0},{8,12},{12,8},{16,20},{20,16},{24,28},{28,24},{32,36},... | collective-permute-start | bytes 5898248 | tf_op jit(solution)/shard_map/ppermute | solution.py:385
  41.0 2.4 %collective-permute-start = (f32[144,768]{1,0:T(8,128)}, f32[144,768]{1,0:T(8,128)S(1)}, u32[]{:S(2)}, u32[]{:S(2)}) collective-permute-start(f32[144,768]{1,0:T(8,128)} %get-tuple-element.60), channel_id=1, source_target_pairs={{0,4},{4,0},{8,12},{12,8},{16,20},{20,16},{24,28},{28,24},{32,36},... | collective-permute-start | bytes 1327112 | tf_op jit(solution)/shard_map/ppermute | solution.py:385
  43.4 16.7 %all-to-all-done.refs_0_ = bf16[16,184,128]{2,1,0:T(8,128)(2,1)S(1)} async-done(((bf16[16,184,128]{2,1,0:T(8,128)(2,1)}), bf16[16,184,128]{2,1,0:T(8,128)(2,1)S(1)}, u32[]{:S(2)}, u32[]{:S(2)}) %all-to-all-start) | async-done | bytes 753696 | tf_op jit(solution)/shard_map/all_to_all | solution.py:377
  60.1 1.2 shard_map.84
  61.3 0.0 collective-permute-done.factor2_ref
  61.3 0.0 collective-permute-done.1.down2_hbm
  61.3 0.0 collective-permute-done.2.gate2_hbm
  61.3 0.0 collective-permute-done.3.up2_hbm
  61.3 23.6 %all_to_all.20.in_ref = bf16[8,368,128]{2,1,0:T(8,128)(2,1)S(1)} all-to-all(bf16[8,368,128]{2,1,0:T(8,128)(2,1)S(1)} %get-tuple-element.64), channel_id=1, replica_groups={{0,8,16,24,32,40,48,56},{4,12,20,28,36,44,52,60},{1,9,17,25,33,41,49,57..., dimensions={0} | all-to-all | bytes 1507328 | tf_op jit(solution)/shard_map/all_to_all | solution.py:380
  85.0 0.0 copy-done
  85.0 5.3 %shard_map.86 = bf16[8,368,128]{2,1,0:T(8,128)(2,1)S(1)} custom-call(bf16[8,368,128]{2,1,0:T(8,128)(2,1)S(1)} %all_to_all.20.in_ref, f32[144,768]{1,0:T(8,128)S(1)} %copy-done, f32[144,768]{1,0:T(8,128)S(1)} %collective-permute-done.factor2_ref, bf16[2560,384]{1,0:T(8,128)(2,1)} %get-tuple-element.67.down_hbm, ...), custom_call_target="tpu_custom_call" | custom-call | tf_op jit(solution)/shard_map/pallas_call | solution.py:352
  90.3 0.0 copy-start.1
  90.3 18.8 %all_to_all.21.refs_0_ = bf16[8,368,128]{2,1,0:T(8,128)(2,1)S(1)} all-to-all(bf16[8,368,128]{2,1,0:T(8,128)(2,1)S(1)} %shard_map.86), channel_id=1, replica_groups={{0,8,16,24,32,40,48,56},{4,12,20,28,36,44,52,60},{1,9,17,25,33,41,49,57..., dimensions={0} | all-to-all | bytes 1507328 | tf_op jit(solution)/shard_map/all_to_all | solution.py:380
  109.1 1.5 %shard_map.87 = bf16[16,184,128]{2,1,0:T(8,128)(2,1)} custom-call(bf16[8,368,128]{2,1,0:T(8,128)(2,1)S(1)} %all_to_all.21.refs_0_, bf16[144,128]{1,0:T(8,128)(2,1)S(1)} %get-tuple-element.73.refs_1_, bf16[144,16]{1,0:T(8,128)(2,1)S(1)} %get-tuple-element.74.refs_2_), custom_call_target="tpu_custom_call" | custom-call | tf_op jit(solution)/shard_map/pallas_call | solution.py:343
  110.6 5.8 %all-to-all-start.3 = ((bf16[16,184,128]{2,1,0:T(8,128)(2,1)}), bf16[16,184,128]{2,1,0:T(8,128)(2,1)S(1)}, u32[]{:S(2)}, u32[]{:S(2)}) async-start(bf16[16,184,128]{2,1,0:T(8,128)(2,1)} %shard_map.87), calls=%async_computation.3 | async-start | bytes 1507328 | tf_op jit(solution)/shard_map/all_to_all | solution.py:377
  116.4 0.0 copy-done.1
  116.4 0.5 shard_map.88
  116.9 27.7 %all-to-all-done.3.in_ref = bf16[16,184,128]{2,1,0:T(8,128)(2,1)S(1)} async-done(((bf16[16,184,128]{2,1,0:T(8,128)(2,1)}), bf16[16,184,128]{2,1,0:T(8,128)(2,1)S(1)}, u32[]{:S(2)}, u32[]{:S(2)}) %all-to-all-start.3) | async-done | bytes 753696 | tf_op jit(solution)/shard_map/all_to_all | solution.py:377
  144.6 1.0 shard_map.89
Async XLA Ops:
  15.1 45.0 %all-to-all-start = ((bf16[16,184,128]{2,1,0:T(8,128)(2,1)}), bf16[16,184,128]{2,1,0:T(8,128)(2,1)S(1)}, u32[]{:S(2)}, u32[]{:S(2)}) async-start(bf16[16,184,128]{2,1,0:T(8,128)(2,1)} %shard_map.82), calls=%async_computation | async-start | bytes 1507328 | tf_op jit(solution)/shard_map/all_to_all | solution.py:377
  34.6 50.4 %copy-start = (f32[144,768]{1,0:T(8,128)S(1)}, f32[144,768]{1,0:T(8,128)}, u32[]{:S(2)}) copy-start(f32[144,768]{1,0:T(8,128)} %get-tuple-element.65.factor_ref) | copy-start | bytes 1327108
  34.6 26.7 %collective-permute-start.1 = (bf16[2560,384]{1,0:T(8,128)(2,1)}, bf16[2560,384]{1,0:T(8,128)(2,1)}, u32[]{:S(2)}, u32[]{:S(2)}) collective-permute-start(bf16[2560,384]{1,0:T(8,128)(2,1)} %get-tuple-element.67.down_hbm), channel_id=1, source_target_pairs={{0,4},{4,0},{8,12},{12,8},{16,20},{20,16},{24,28},{28,24},{32,36},... | collective-permute-start | bytes 5898248 | tf_op jit(solution)/shard_map/ppermute | solution.py:385
  36.7 24.6 %collective-permute-start.2 = (bf16[384,2560]{1,0:T(8,128)(2,1)}, bf16[384,2560]{1,0:T(8,128)(2,1)}, u32[]{:S(2)}, u32[]{:S(2)}) collective-permute-start(bf16[384,2560]{1,0:T(8,128)(2,1)} %get-tuple-element.69.gate_hbm), channel_id=1, source_target_pairs={{0,4},{4,0},{8,12},{12,8},{16,20},{20,16},{24,28},{28,24},{32,36},... | collective-permute-start | bytes 5898248 | tf_op jit(solution)/shard_map/ppermute | solution.py:385
  39.1 22.2 %collective-permute-start.3 = (bf16[384,2560]{1,0:T(8,128)(2,1)}, bf16[384,2560]{1,0:T(8,128)(2,1)}, u32[]{:S(2)}, u32[]{:S(2)}) collective-permute-start(bf16[384,2560]{1,0:T(8,128)(2,1)} %get-tuple-element.70.up_hbm), channel_id=1, source_target_pairs={{0,4},{4,0},{8,12},{12,8},{16,20},{20,16},{24,28},{28,24},{32,36},... | collective-permute-start | bytes 5898248 | tf_op jit(solution)/shard_map/ppermute | solution.py:385
  41.0 20.3 %collective-permute-start = (f32[144,768]{1,0:T(8,128)}, f32[144,768]{1,0:T(8,128)S(1)}, u32[]{:S(2)}, u32[]{:S(2)}) collective-permute-start(f32[144,768]{1,0:T(8,128)} %get-tuple-element.60), channel_id=1, source_target_pairs={{0,4},{4,0},{8,12},{12,8},{16,20},{20,16},{24,28},{28,24},{32,36},... | collective-permute-start | bytes 1327112 | tf_op jit(solution)/shard_map/ppermute | solution.py:385
  90.3 26.2 %copy-start.1 = (s32[24,3]{0,1:T(4,128)S(1)}, s32[24,3]{0,1:T(4,128)}, u32[]{:S(2)}) copy-start(s32[24,3]{0,1:T(4,128)} %param.9) | copy-start | bytes 868
  110.6 34.0 %all-to-all-start.3 = ((bf16[16,184,128]{2,1,0:T(8,128)(2,1)}), bf16[16,184,128]{2,1,0:T(8,128)(2,1)S(1)}, u32[]{:S(2)}, u32[]{:S(2)}) async-start(bf16[16,184,128]{2,1,0:T(8,128)(2,1)} %shard_map.87), calls=%async_computation.3 | async-start | bytes 1507328 | tf_op jit(solution)/shard_map/all_to_all | solution.py:377
